TPU v7x, 128 devices: a whole 4x4x4 slice. The times are simulated.
128 devices in a mesh: seq: 16 (over x_lo, z, core), tp: 8 (over y, x_hi).
Axes of the slice: x: 4 (x_hi: 2, x_lo: 2; x = x_hi * 2 + x_lo), y: 4, z: 4, core: 2. Of those that a mesh axis runs over, the one named last changes fastest.
Arguments:
- prompt_x: bfloat16 [8192, 8192], P('seq'), may hold values from -40 to 40
- w_query: bfloat16 [8192, 4096], P(None, 'tp'), may hold values from -0.0625 to 0.0625
- w_key: bfloat16 [8192, 1024], P(None, 'tp'), may hold values from -0.0625 to 0.0625
- w_value: bfloat16 [8192, 1024], P(None, 'tp'), may hold values from -0.0625 to 0.0625
- decode_x: bfloat16 [4, 256, 8192], P(None, 'seq', 'tp'), may hold values from -40 to 40
- cache_keys: bfloat16 [256, 256, 1024], P('seq', None, 'tp'), may hold values from -6 to 6
- cache_values: bfloat16 [256, 256, 1024], P('seq', None, 'tp'), may hold values from -6 to 6
- cache_len: int32 [256], P('seq'), may hold values from 1 to 256, as said below
- prompt_blocks: int32 [256], P('seq'), may hold values from 1 to 16, as said below
Outputs:
- prefill_out: bfloat16 [8192, 4096], P('seq', 'tp')
- decode_out: bfloat16 [4, 256, 4096], P(None, 'seq', 'tp')
Inputs may be any that keep to these rules, and one draw needn't show every extreme that they name: `cache_len`: some row reaches 256. `prompt_blocks`: some row takes all 16 blocks.
All inputs are finite; a program needn't handle non-finite values.
Results may differ from a plain program's by a relative error of at most 0.015.
The roundings to bfloat16 on the way count: a program that leaves them out, or rounds other values in their place, can miss the bound.
Values may be sent and summed in bfloat16 or wider, within the bound.
A program may use at most 256 MiB of HBM per device.

v0:
```python
from functools import reduce
import math

import jax
import jax.numpy as jnp
from jax import lax
from jax.sharding import PartitionSpec as P

G = 4
DH = 128


theta_base = 500000.0
neg_big = -1e30


def rotate(values, positions):
    half_size = values.shape[-1] // 2
    index_float = jnp.arange(half_size, dtype=jnp.float32)
    frequency = jnp.exp(index_float * (-2.0 / values.shape[-1] * math.log(theta_base)))
    angle = positions[..., None] * frequency
    cosine = jnp.cos(angle)
    sine_part = jnp.sin(angle)
    first_half = values[..., :half_size]
    second_half = values[..., half_size:]
    return jnp.concatenate(
        [
            first_half * cosine - second_half * sine_part,
            second_half * cosine + first_half * sine_part,
        ],
        axis=-1,
    )


def attend_block(state, queries, keys_block, values_block, allowed):
    running_max, running_sum, running_out = state
    scores = jnp.einsum(
        "thgd,shd->thgs", queries, keys_block, preferred_element_type=jnp.float32
    ) * DH ** (-0.5)
    mask_full = allowed[:, None, None, :]
    scores = jnp.where(mask_full, scores, neg_big)
    new_max = jnp.maximum(running_max, scores.max(-1))
    weights = jnp.where(mask_full, jnp.exp(scores - new_max[..., None]), 0.0)
    new_sum = weights.sum(-1)
    new_out = jnp.einsum(
        "thgs,shd->thgd",
        weights.astype(jnp.bfloat16),
        values_block,
        preferred_element_type=jnp.float32,
    )
    return (new_max, new_sum, new_out)


def partial_softmax(parts):
    masked = [jnp.where(piece_info[1], piece_info[0], neg_big) for piece_info in parts]
    top_score = reduce(jnp.maximum, [scored.max(-1) for scored in masked])
    weights = [
        jnp.where(piece_info[1], jnp.exp(scored - top_score[..., None]), 0.0)
        for scored, piece_info in zip(masked, parts)
    ]
    weight_sum = sum((weight_part.sum(-1) for weight_part in weights))
    mixed_sum = sum(
        (
            jnp.einsum(
                piece_info[3],
                weight_part.astype(jnp.bfloat16),
                piece_info[2],
                preferred_element_type=jnp.float32,
            )
            for weight_part, piece_info in zip(weights, parts)
        )
    )
    return (top_score, weight_sum, mixed_sum)


def body(
    prompt_x, w_query, w_key, w_value, decode_x, cache_keys, cache_values, cache_len, prompt_blocks
):
    tok_rows = prompt_x.shape[0]
    head_count = w_key.shape[1] // DH
    scale_factor = DH ** (-0.5)
    seq_index = lax.axis_index("seq")
    own_pos = seq_index * tok_rows + jnp.arange(tok_rows, dtype=jnp.int32)
    own_float = own_pos.astype(jnp.float32)
    queries = rotate(
        jnp.dot(prompt_x, w_query, preferred_element_type=jnp.float32).reshape(
            tok_rows, head_count, G, DH
        ),
        own_float[:, None, None],
    ).astype(jnp.bfloat16)
    keys_own = rotate(
        jnp.dot(prompt_x, w_key, preferred_element_type=jnp.float32).reshape(
            tok_rows, head_count, DH
        ),
        own_float[:, None],
    ).astype(jnp.bfloat16)
    values_own = (
        jnp.dot(prompt_x, w_value, preferred_element_type=jnp.float32)
        .reshape(tok_rows, head_count, DH)
        .astype(jnp.bfloat16)
    )
    state_init = (
        jnp.full((tok_rows, head_count, G), neg_big, jnp.float32),
        jnp.zeros((tok_rows, head_count, G), jnp.float32),
        jnp.zeros((tok_rows, head_count, G, DH), jnp.float32),
    )
    piece_pair = (
        lax.all_gather(keys_own, "seq", axis=0, tiled=True),
        lax.all_gather(values_own, "seq", axis=0, tiled=True),
    )
    block_pos = jnp.arange(piece_pair[0].shape[0], dtype=jnp.int32)
    final_state = attend_block(
        state_init, queries, piece_pair[0], piece_pair[1], block_pos[None, :] <= own_pos[:, None]
    )
    prefill_out = (
        (final_state[2] / final_state[1][..., None])
        .astype(jnp.bfloat16)
        .reshape(tok_rows, head_count * G * DH)
    )
    steps_count, row_count, part_width = decode_x.shape
    weights_all = (w_query, w_key, w_value)
    piece_rows = lax.all_gather(decode_x, "tp", axis=2, tiled=True)
    flat_rows = piece_rows.reshape(steps_count * row_count, piece_rows.shape[2])
    dec_q, dec_k, dec_v = tuple(
        (jnp.dot(flat_rows, weight, preferred_element_type=jnp.float32) for weight in weights_all)
    )
    base_pos = prompt_blocks * tok_rows + cache_len
    new_pos = (base_pos[None, :] + jnp.arange(steps_count, dtype=jnp.int32)[:, None]).astype(
        jnp.float32
    )
    dec_q = rotate(
        dec_q.reshape(steps_count, row_count, head_count, G, DH), new_pos[:, :, None, None]
    ).astype(jnp.bfloat16)
    dec_k = rotate(
        dec_k.reshape(steps_count, row_count, head_count, DH), new_pos[:, :, None]
    ).astype(jnp.bfloat16)
    dec_v = dec_v.reshape(steps_count, row_count, head_count, DH).astype(jnp.bfloat16)
    slot_count = cache_keys.shape[1]
    cache_k4 = cache_keys.reshape(row_count, slot_count, head_count, DH)
    cache_v4 = cache_values.reshape(row_count, slot_count, head_count, DH)
    cache_scores = (
        jnp.einsum("trhgd,rlhd->trhgl", dec_q, cache_k4, preferred_element_type=jnp.float32)
        * scale_factor
    )
    cache_mask = (jnp.arange(slot_count, dtype=jnp.int32)[None, :] < cache_len[:, None])[
        None, :, None, None, :
    ]
    new_scores = (
        jnp.einsum("trhgd,urhd->trhgu", dec_q, dec_k, preferred_element_type=jnp.float32)
        * scale_factor
    )
    new_mask = (
        jnp.arange(steps_count, dtype=jnp.int32)[None, :]
        <= jnp.arange(steps_count, dtype=jnp.int32)[:, None]
    )[:, None, None, None, :]
    local_parts = [
        (cache_scores, cache_mask, cache_v4, "trhgl,rlhd->trhgd"),
        (new_scores, new_mask, dec_v, "trhgu,urhd->trhgd"),
    ]
    prompt_keys, prompt_values = (
        lax.all_gather(keys_own, "seq", axis=0, tiled=True),
        lax.all_gather(values_own, "seq", axis=0, tiled=True),
    )
    prompt_scores = (
        jnp.einsum("trhgd,phd->trhgp", dec_q, prompt_keys, preferred_element_type=jnp.float32)
        * scale_factor
    )
    prompt_mask = (
        jnp.arange(prompt_keys.shape[0], dtype=jnp.int32)[None, :]
        < (prompt_blocks * tok_rows)[:, None]
    )[None, :, None, None, :]
    top_score, weight_sum, mixed_sum = partial_softmax(
        [(prompt_scores, prompt_mask, prompt_values, "trhgp,phd->trhgd")] + local_parts
    )
    decode_out = (
        (mixed_sum / weight_sum[..., None])
        .astype(jnp.bfloat16)
        .reshape(steps_count, row_count, head_count * G * DH)
    )
    return (prefill_out, decode_out)


def solution(mesh):
    placed = (
        P("seq", None),
        P(None, "tp"),
        P(None, "tp"),
        P(None, "tp"),
        P(None, "seq", "tp"),
        P("seq", None, "tp"),
        P("seq", None, "tp"),
        P("seq"),
        P("seq"),
    )
    return jax.shard_map(
        body,
        mesh=mesh,
        in_specs=placed,
        out_specs=(P("seq", "tp"), P(None, "seq", "tp")),
        check_vma=False,
    )
```

profile of v0, /device:TPU:1, one launch (start us, length us, event | category | flops | bytes accessed | tf_op | source)
XLA Modules:
  0.0 201.1 jit_solution(13253828330444166132)
XLA Ops:
  7.2 0.0 all-gather.7.cloned.1.call-start
  7.2 0.7 all-gather.7.cloned.1.call-update
  7.9 0.0 all-gather.5.cloned.1.call-start
  8.0 0.8 copy-done
  8.8 6.3 %convolution_bitcast_fusion = f32[512,1,128]{0,2,1:T(8,128)S(1)} fusion(bf16[512,8192]{1,0:T(8,128)(2,1)} %param.9, bf16[8192,128]{1,0:T(8,128)(2,1)S(1)} %copy-done), kind=kOutput, calls=%fused_computation.32 | convolution fusion | flops 1073741824 | bytes 10747904 | tf_op jit(solution)/shard_map/dot_general | solution.py:92
  15.0 0.6 fusion.88
  15.6 0.7 pad_maximum_fusion
  16.3 0.0 all-gather.9.cloned.1.call-start
  16.3 7.0 %convolution_convert_fusion = bf16[512,128]{1,0:T(8,128)(2,1)} fusion(bf16[512,8192]{1,0:T(8,128)(2,1)} %param.9, bf16[8192,128]{1,0:T(8,128)(2,1)} %param.12), kind=kOutput, calls=%fused_computation.33 | convolution fusion | flops 1073807360 | bytes 10616832 | tf_op jit(solution)/shard_map/dot_general | solution.py:98
  23.3 2.0 multiply_cosine_fusion
  25.3 5.5 %iota_compare_fusion = pred[512,8192]{0,1:T(8,128)(4,1)} fusion(s32[512]{0:T(512)S(1)} %iota_add_fusion), kind=kLoop, calls=%fused_computation.8 | loop fusion | flops 4194304 | bytes 4196352 | tf_op jit(solution)/shard_map/le | solution.py:113
  30.8 9.5 %fusion.129 = f32[512,512]{0,1:T(8,128)S(1)} fusion(bf16[512,8192]{1,0:T(8,128)(2,1)} %param.9, bf16[8192,512]{1,0:T(8,128)(2,1)} %param.10), kind=kOutput, calls=%fused_computation.133 | convolution fusion | flops 4294967296 | bytes 17825792 | tf_op jit(solution)/shard_map/dot_general | solution.py:86
  40.3 1.1 fusion.125
  41.3 1.4 copy.104
  42.7 2.3 %copy.103 = f32[512,1,4,64]{3,0,2,1:T(8,128)} copy(f32[512,1,4,64]{0,3,2,1:T(8,128)} %get-tuple-element.13) | data formatting | bytes 1048576
  45.1 11.4 %copy.98 = bf16[512,8192]{1,0:T(8,128)(2,1)} copy(bf16[512,8192]{0,1:T(8,128)(2,1)} %bitcast.205) | data formatting | bytes 16777216 | tf_op jit(solution)/shard_map/reshape.252
  56.5 0.1 iota_compare_fusion.2
  56.6 0.8 multiply_cosine_fusion.3
  57.4 0.1 iota_compare_fusion.1
  57.6 2.5 %fusion.74 = (bf16[512,4,64]{2,0,1:T(8,128)(2,1)}, bf16[512,4,64]{2,0,1:T(8,128)(2,1)}) fusion(f32[512,1,4,64]{3,0,2,1:T(8,128)S(1)} %copy.104, f32[512,1,4,64]{3,0,2,1:T(8,128)} %copy.103, f32[512,64]{1,0:T(8,128)} %get-tuple-element.23, f32[512,64]{1,0:T(8,128)S(1)} %get-tuple-element.22), kind=kLoop, calls=%fused_computation.55 | loop fusion | flops 1048576 | bytes 1835008 | tf_op jit(solution)/shard_map/concatenate | solution.py:26
  60.1 1.7 fusion.60
  61.9 0.2 fusion.115
  62.1 6.4 %convolution_bitcast_fusion.1 = f32[4,16,1,4,128]{4,1,3,0,2:T(8,128)S(1)} fusion(bf16[4,128,8192,1]{2,1,0,3:T(8,128)(2,1)} %bitcast.206, bf16[4,16,8192]{2,1,0:T(8,128)(2,1)} %all-gather.7.cloned.1.call-done), kind=kOutput, calls=%fused_computation.38 | convolution fusion | flops 536870912 | bytes 9568256 | tf_op jit(solution)/shard_map/dot_general | solution.py:125
  68.5 0.1 fusion.97
  68.6 0.1 pad_maximum_fusion.1
  68.8 0.1 maximum_bitcast_fusion
  68.8 1.4 fusion.126
  70.2 0.1 copy.73
  70.3 2.4 %fusion.128 = (f32[4,16,4]{2,0,1:T(4,128)}, f32[4,16,1,4,256]{4,3,0,1,2:T(4,128)S(1)}) fusion(bf16[16,256,128]{2,1,0:T(8,128)(2,1)} %param.14, bf16[4,16,4,128]{3,1,2,0:T(8,128)(2,1)} %copy-done.2, pred[16,256]{1,0:T(8,128)(4,1)S(1)} %iota_compare_fusion.2), kind=kOutput, calls=%fused_computation.132 | convolution fusion | flops 16973568 | bytes 1381376 | tf_op jit(solution)/shard_map/trhgd,rlhd->trhgl/dot_general | solution.py:142
  72.7 1.4 copy.70
  74.1 2.7 %fusion.66 = bf16[4,16,128,1]{2,1,0,3:T(8,128)(2,1)} fusion(bf16[4,16,8192]{2,1,0:T(8,128)(2,1)S(1)} %copy-done.1, bf16[8192,128]{1,0:T(8,128)(2,1)} %param.12), kind=kOutput, calls=%fused_computation.46 | convolution fusion | flops 134225920 | bytes 3162112 | tf_op jit(solution)/shard_map/dot_general | solution.py:125
  76.8 18.2 %all-gather.5.cloned.1.call-done = bf16[8192,1,128]{0,2,1:T(8,128)(2,1)} async-done(((bf16[512,1,128]{0,2,1:T(8,128)(2,1)}), bf16[8192,1,128]{0,2,1:T(8,128)(2,1)}) %all-gather.5.cloned.1.call-update) | async-done | bytes 2097168 | tf_op jit(solution)/shard_map/all_gather | solution.py:108
  94.9 28.7 %fusion = (f32[512,4]{0,1:T(4,128)S(1)}, f32[8192,512,4]{1,0,2:T(8,128)}) fusion(pred[512,8192]{0,1:T(8,128)(4,1)} %iota_compare_fusion, bf16[512,4,64]{2,0,1:T(8,128)(2,1)} %get-tuple-element.11, bf16[512,4,64]{2,0,1:T(8,128)(2,1)} %get-tuple-element.10, bf16[8192,1,128]{0,2,1:T(8,128)(2,1)} %all-gather.5.cloned.1.call-done), kind=kOutput, calls=%fused_computation.2 | convolution fusion | flops 4346345472 | bytes 73932800 | tf_op jit(solution)/shard_map/thgd,shd->thgs/dot_general | solution.py:37
  123.7 22.9 %fusion.1 = f32[512,4]{0,1:T(4,128)S(1)} fusion(f32[8192,512,4]{1,0,2:T(8,128)} %get-tuple-element.27, f32[512,4]{0,1:T(4,128)S(1)} %broadcast_maximum_fusion, pred[512,8192]{0,1:T(8,128)(4,1)} %iota_compare_fusion), kind=kLoop, calls=%fused_computation.3 | loop fusion | flops 83884032 | bytes 71319552 | tf_op jit(solution)/shard_map/reduce_sum | solution.py:44
  146.6 0.0 all-gather.9.cloned.1.call-done
  146.6 26.7 %divide_convert_fusion = bf16[1,128,512,4]{2,1,3,0:T(8,128)(2,1)S(1)} fusion(f32[512,4]{0,1:T(4,128)S(1)} %fusion.1, f32[8192,512,4]{1,0,2:T(8,128)} %get-tuple-element.27, f32[512,4]{0,1:T(4,128)S(1)} %broadcast_maximum_fusion, pred[512,8192]{0,1:T(8,128)(4,1)} %iota_compare_fusion, bf16[8192,128]{1,0:T(8,128)(2,1)} %all-gather.9.cloned.1.call-done), kind=kOutput, calls=%fused_computation.52 | convolution fusion | flops 4379377664 | bytes 73940992 | tf_op jit(solution)/shard_map/thgs,shd->thgd/dot_general | solution.py:45
  173.3 1.0 copy.83
  174.3 6.3 %fusion.127 = (f32[4,16,4]{1,2,0:T(4,128)S(1)}, f32[4,16,1,4,8192]{4,1,3,0,2:T(8,128)}) fusion(bf16[4,16,4,128]{3,1,2,0:T(8,128)(2,1)S(1)} %copy-done.3, bf16[8192,1,128]{0,2,1:T(8,128)(2,1)} %all-gather.5.cloned.1.call-done, pred[16,8192]{1,0:T(8,128)(4,1)S(1)} %iota_compare_fusion.1), kind=kOutput, calls=%fused_computation.131 | convolution fusion | flops 543162112 | bytes 10683392 | tf_op jit(solution)/shard_map/trhgd,phd->trhgp/dot_general | solution.py:165
  180.7 0.1 copy.74
  180.8 0.2 fusion.94
  181.0 0.3 fusion.99
  181.3 0.3 fusion.83
  181.6 1.6 fusion.70
  183.1 0.1 copy.81
  183.2 5.2 %fusion.9 = f32[4,16,4]{1,2,0:T(4,128)S(1)} fusion(f32[4,16,1,4,8192]{4,1,3,0,2:T(8,128)} %get-tuple-element.31, f32[4,16,4]{1,2,0:T(4,128)S(1)} %bitcast.210, pred[16,8192]{1,0:T(8,128)(4,1)S(1)} %iota_compare_fusion.1), kind=kLoop, calls=%fused_computation.13 | loop fusion | flops 6291200 | bytes 8521728 | tf_op jit(solution)/shard_map/reduce_sum | solution.py:61
  188.4 0.1 copy.80
  188.5 5.4 %fusion.55 = bf16[4,16,1,4,128]{4,1,3,0,2:T(8,128)(2,1)S(1)} fusion(f32[4,16,1,4,8192]{4,1,3,0,2:T(8,128)} %get-tuple-element.31, f32[4,16,4]{1,2,0:T(4,128)S(1)} %bitcast.211, pred[16,8192]{1,0:T(8,128)(4,1)S(1)} %iota_compare_fusion.1, bf16[8192,128]{1,0:T(8,128)(2,1)} %all-gather.9.cloned.1.call-done, f32[16,128,4,4]{1,3,2,0:T(4,128)S(1)} %fusion.99, ...), kind=kOutput, calls=%fused_computation.43 | convolution fusion | flops 543293440 | bytes 10946560 | tf_op jit(solution)/shard_map/trhgp,phd->trhgd/dot_general | solution.py:64
  193.9 0.7 reshape.540
  (34 shorter events, 0.2 us)
Async XLA Ops:
  7.2 1.6 copy-start
  7.2 52.9 %all-gather.7.cloned.1.call-start = ((), (), s32[]{:S(2)}) async-start(), calls=%async_computation.1 | async-start | bytes 1179648 | tf_op jit(solution)/shard_map/all_gather | solution.py:122
  7.9 87.0 %all-gather.5.cloned.1.call-start = ((), (), s32[]{:S(2)}) async-start(), calls=%async_computation | async-start | bytes 2228224 | tf_op jit(solution)/shard_map/all_gather | solution.py:108
  16.3 130.3 %all-gather.9.cloned.1.call-start = ((), (), s32[]{:S(2)}) async-start(), calls=%async_computation.2 | async-start | bytes 2228224 | tf_op jit(solution)/shard_map/all_gather | solution.py:109
  45.1 11.5 %copy-start.9 = (s32[16]{0:T(128)S(1)}, s32[16]{0:T(128)}, u32[]{:S(2)}) copy-start(s32[16]{0:T(128)} %param.16) | copy-start | bytes 196
  45.1 11.5 %copy-start.10 = (s32[16]{0:T(128)S(1)}, s32[16]{0:T(128)}, u32[]{:S(2)}) copy-start(s32[16]{0:T(128)} %param.17) | copy-start | bytes 196
  61.8 6.7 %copy-start.4 = (f32[4,16,64]{2,1,0:T(8,128)S(1)}, f32[4,16,64]{2,1,0:T(8,128)}, u32[]{:S(2)}) copy-start(f32[4,16,64]{2,1,0:T(8,128)} %get-tuple-element.20) | copy-start | bytes 49156
  61.9 6.7 %copy-start.5 = (f32[4,16,64]{2,1,0:T(8,128)S(1)}, f32[4,16,64]{2,1,0:T(8,128)}, u32[]{:S(2)}) copy-start(f32[4,16,64]{2,1,0:T(8,128)} %get-tuple-element.21) | copy-start | bytes 49156
  62.1 12.0 %copy-start.1 = (bf16[4,16,8192]{2,1,0:T(8,128)(2,1)S(1)}, bf16[4,16,8192]{2,1,0:T(8,128)(2,1)}, u32[]{:S(2)}) copy-start(bf16[4,16,8192]{2,1,0:T(8,128)(2,1)} %all-gather.7.cloned.1.call-done) | copy-start | bytes 3145732
  68.7 1.5 copy-start.2
  146.6 27.8 %copy-start.3 = (bf16[4,16,4,128]{3,1,2,0:T(8,128)(2,1)S(1)}, bf16[4,16,4,128]{3,1,2,0:T(8,128)(2,1)}, u32[]{:S(2)}) copy-start(bf16[4,16,4,128]{3,1,2,0:T(8,128)(2,1)} %copy-done.2) | copy-start | bytes 196612
  174.3 6.3 %copy-start.7 = (f32[4,16,4]{1,2,0:T(4,128)S(1)}, f32[4,16,4]{1,2,0:T(4,128)}, u32[]{:S(2)}) copy-start(f32[4,16,4]{1,2,0:T(4,128)} %copy.70) | copy-start | bytes 3076
  174.3 6.5 %copy-start.6 = (f32[4,16,1,4,4]{3,4,0,1,2:T(4,128)S(1)}, f32[4,16,1,4,4]{3,4,0,1,2:T(4,128)}, u32[]{:S(2)}) copy-start(f32[4,16,1,4,4]{3,4,0,1,2:T(4,128)} %get-tuple-element.29) | copy-start | bytes 12292
  174.3 6.6 %copy-start.8 = (bf16[4,16,128,1]{2,1,0,3:T(8,128)(2,1)S(1)}, bf16[4,16,128,1]{2,1,0,3:T(8,128)(2,1)}, u32[]{:S(2)}) copy-start(bf16[4,16,128,1]{2,1,0,3:T(8,128)(2,1)} %fusion.66) | copy-start | bytes 49156
Sparse Core Ops, SparseCore 0:
  10.3 48.0 all-gather.6
  60.1 34.8 all-gather.4
  96.7 34.0 all-gather.8
where the time goes:
time: 202 us; the launch traced here: 201 us
  matrix products  106 us (52%)
  other arithmetic  41.4 us (20%)
  local copies, waits for them, and re-layouts  20.6 us (10%)
  waiting for transfers between devices  18.9 us (9%)
  between operations  14 us (7%)
    dot_general x1, matrix products, attend_block(): jnp.einsum('thgd,shd->thgs', queries, keys_block, preferred_element_type=...  28.7 us
    dot_general x1, matrix products, attend_block(): jnp.einsum('thgs,shd->thgd', weights.astype(jnp.bfloat16), values_block,...  26.7 us
    reduce_sum x1, other arithmetic, attend_block(): new_sum = weights.sum(-1)  22.9 us
    all_gather x1, waiting for transfers between devices, body(): lax.all_gather(keys_own, 'seq', axis=0, tiled=True)  18.2 us
    another operation x1, local copies, waits for them, and re-layouts  11.4 us
    dot_general x3, matrix products, body(): jnp.dot(flat_rows, weight, preferred_element_type=jnp.float32)  10.8 us
    dot_general x1, matrix products, body(): jnp.dot(prompt_x, w_query, preferred_element_type=jnp.float32)  9.47 us
    dot_general x3, matrix products, partial_softmax(): jnp.einsum(piece_info[3], weight_part.astype(jnp.bfloat16), piece_info[2]...  7.23 us
  transfers between devices with their start and end apart: 3, of which 1 were waited for; matrix products, arithmetic and copies ran while one was open for 59% of the time, Pallas kernels for 0%

commit v1 on v0

v1 whole, which is shorter than its diff:
```python
import functools
import math

import jax
import jax.numpy as jnp
import numpy as np
from jax import lax
from jax.experimental import pallas as pl
from jax.experimental.pallas import tpu as pltpu
from jax.sharding import PartitionSpec as P

G = 4
DH = 128
HALF = DH // 2
TOK = 512
KC = 8
KW = 1024
ROWS = 16
STEPS = 4
DQ = STEPS * ROWS * G
TILE = 256
THETA = 500000.0
NEG = -1e30
BIG = 1e30
SC = DH**-0.5 * math.log2(math.e)
BF = jnp.bfloat16
F32 = jnp.float32
MESH = pl.DeviceIdType.MESH


def rope(a, cos, sin):
    return a * cos + pltpu.roll(a, HALF, axis=1) * sin


def dot(a, b):
    return jnp.dot(a, b, preferred_element_type=F32)


def scores(q, k):
    return lax.dot_general(q, k, (((1,), (1,)), ((), ())), preferred_element_type=F32)


def kernel(
    px, wq, wk, wv, dx, ck, cv, clen, pblk, freq, po, do,
    xb, wkv, wqb, kall, vall, xd, ckb, cvb, qs, qd, kd, vd,
    m_s, l_s, acc, accq, acckv, accd, cos_s, sin_s,
    sx, swk, swv, swq, sc, sdx, ss, rk, rv, ssx, rx,
):
    seq = lax.axis_index("seq")
    tp = lax.axis_index("tp")
    core = seq % 2
    chip = seq // 2
    z = chip % 4
    xl = chip // 4

    def at(dxl, dz):
        return ((xl + dxl) % 2) * 4 + (z + dz) % 4

    s_zm = at(0, 3) * 2 + core
    s_zp = at(0, 1) * 2 + core
    s_x = at(1, 0) * 2 + core
    s_zz = at(0, 2) * 2 + core
    s_sib = chip * 2 + (1 - core)
    t_x = (tp // 2) * 2 + (1 - tp % 2)
    t_ym = (tp + 6) % 8
    t_yp = (tp + 2) % 8

    def in_x(c):
        return pltpu.make_async_copy(px.at[:, pl.ds(c * KW, KW)], xb.at[c], sx.at[c])

    def in_wk(c):
        return pltpu.make_async_copy(wk.at[pl.ds(c * KW, KW)], wkv.at[c, :, pl.ds(0, DH)], swk.at[c])

    def in_wv(c):
        return pltpu.make_async_copy(wv.at[pl.ds(c * KW, KW)], wkv.at[c, :, pl.ds(DH, DH)], swv.at[c])

    def in_wq(c):
        return pltpu.make_async_copy(wq.at[pl.ds(c * KW, KW)], wqb.at[c], swq.at[c])

    in_ck = pltpu.make_async_copy(ck, ckb, sc.at[0])
    in_cv = pltpu.make_async_copy(cv, cvb.at[:, :, pl.ds(0, DH)], sc.at[1])
    in_dx = pltpu.make_async_copy(dx, xd.at[tp], sdx)

    barrier = pltpu.get_barrier_semaphore()
    for dev in ((s_zm, tp), (s_zp, tp), (s_x, tp), (s_sib, tp), (seq, t_x), (seq, t_ym), (seq, t_yp)):
        pl.semaphore_signal(barrier, inc=1, device_id=dev, device_id_type=MESH)
    in_dx.start()
    for c in range(KC):
        in_x(c).start()
        in_wk(c).start()
        in_wv(c).start()

    def send_x(p, dev, i):
        return pltpu.make_async_remote_copy(
            src_ref=xd.at[p], dst_ref=xd.at[p], send_sem=ssx.at[i], recv_sem=rx.at[p],
            device_id=(seq, dev), device_id_type=MESH,
        )

    def send_k(b, dev, i):
        return pltpu.make_async_remote_copy(
            src_ref=kall.at[b], dst_ref=kall.at[b], send_sem=ss.at[i], recv_sem=rk.at[b],
            device_id=(dev, tp), device_id_type=MESH,
        )

    def send_v(b, dev, i):
        ref = vall.at[b, :, pl.ds(0, DH)]
        return pltpu.make_async_remote_copy(
            src_ref=ref, dst_ref=ref, send_sem=ss.at[i], recv_sem=rv.at[b],
            device_id=(dev, tp), device_id_type=MESH,
        )

    def got_k(b):
        send_k(b, s_sib, 0).wait_recv()

    def got_v(b):
        send_v(b, s_sib, 0).wait_recv()

    in_dx.wait()
    pl.semaphore_wait(barrier, 7)
    p_x, p_ym, p_yp = t_x, t_ym, t_yp
    x_first = [send_x(tp, t_x, 0), send_x(tp, t_yp, 1), send_x(tp, t_ym, 2)]
    for cp in x_first:
        cp.start()

    lane = lax.broadcasted_iota(jnp.int32, (1, DH), 1)
    sign = jnp.where(lane < HALF, -1.0, 1.0).astype(F32)
    fr = freq[...]
    pos = (lax.broadcasted_iota(jnp.int32, (TOK, DH), 0) + seq * TOK).astype(F32)
    cos_s[...] = jnp.cos(pos * fr)
    sin_s[...] = jnp.sin(pos * fr) * sign
    vall[:, :, pl.ds(DH, DH)] = jnp.ones((16, TOK, DH), BF)
    cvb[:, :, pl.ds(DH, DH)] = jnp.ones((ROWS, 256, DH), BF)
    vd[:, pl.ds(DH, DH)] = jnp.ones((STEPS * ROWS, DH), BF)

    acckv[...] = jnp.zeros_like(acckv)

    def kv_step(c, _):
        in_x(c).wait()
        in_wk(c).wait()
        in_wv(c).wait()

        @pl.when(c >= KC // 2)
        def _():
            in_wq(2 * c - KC).start()
            in_wq(2 * c - KC + 1).start()

        acckv[...] += dot(xb[c], wkv[c])
        return 0

    lax.fori_loop(0, KC, kv_step, 0)
    in_ck.start()
    in_cv.start()
    kall[seq] = rope(acckv[:, :DH], cos_s[...], sin_s[...]).astype(BF)
    vall[seq, :, pl.ds(0, DH)] = acckv[:, DH:].astype(BF)
    for i, dev in enumerate((s_zp, s_zm, s_x, s_sib)):
        send_k(seq, dev, i).start()
    for i, dev in enumerate((s_zm, s_zp, s_x, s_sib)):
        send_v(seq, dev, 4 + i).start()

    got_x = lambda p: send_x(p, t_x, 0).wait_recv()
    got_x(p_x)
    x_second = [send_x(p_x, t_yp, 3), send_x(p_x, t_ym, 4)]
    for cp in x_second:
        cp.start()
    got_x(p_ym)
    x_third = send_x(p_ym, t_yp, 5)
    x_third.start()

    accq[...] = jnp.zeros_like(accq)

    def q_step(c, _):
        in_wq(c).wait()
        accq[...] += dot(xb[c], wqb[c])
        return 0

    lax.fori_loop(0, KC, q_step, 0)
    for g in range(G):
        qs[pl.ds(g * TOK, TOK), :] = rope(
            accq[:, g * DH : (g + 1) * DH], cos_s[...], sin_s[...]
        ).astype(BF)

    p_bp = (t_yp // 2) * 2 + (1 - tp % 2)
    p_bm = (t_ym // 2) * 2 + (1 - tp % 2)
    got_x(p_bp)
    x_fourth = send_x(p_bp, t_ym, 6)
    x_fourth.start()
    got_k(s_zm)
    send_k(s_zm, s_zp, 8).start()
    got_v(s_zp)
    send_v(s_zp, s_zm, 9).start()
    got_k(s_x)
    send_k(s_x, s_zm, 10).start()
    send_k(s_x, s_zp, 11).start()
    got_v(s_x)
    send_v(s_x, s_zm, 12).start()
    send_v(s_x, s_zp, 13).start()
    got_v(s_zm)
    got_k(s_zp)
    order = ((0, 0), (0, 3), (0, 1), (1, 0), (0, 2), (1, 3), (1, 1), (1, 2))

    def to_sib(n, start):
        b = at(*order[n]) * 2 + core
        for cp in (send_k(b, s_sib, 14 + 2 * n), send_v(b, s_sib, 15 + 2 * n)):
            if start:
                cp.start()
            else:
                cp.wait_send()

    for n in (1, 2, 3):
        to_sib(n, True)

    def prefill_chunk(c, first):
        k = kall[pl.ds(2 * c, 2)].reshape(2 * TOK, DH)
        v = vall[pl.ds(2 * c, 2)].reshape(2 * TOK, 2 * DH)
        count = G * TOK // TILE
        if first:
            row = lax.broadcasted_iota(jnp.int32, (TILE, 2 * TOK), 0) + core * TOK
            col = lax.broadcasted_iota(jnp.int32, (TILE, 2 * TOK), 1)
            masks = [col <= row + h * TILE for h in range(TOK // TILE)]
        rows = [pl.ds(u * TILE, TILE) for u in range(count)]
        s_next = scores(qs[rows[0], :], k)
        outs = []
        for u in range(count):
            s = s_next
            if u + 1 < count:
                s_next = scores(qs[rows[u + 1], :], k)
            if first:
                s = jnp.where(masks[u % (TOK // TILE)], s, NEG)
            top = jnp.broadcast_to(jnp.max(s, axis=1, keepdims=True) * SC, (TILE, DH))
            if not first:
                old = m_s[rows[u], :]
                top = jnp.maximum(old, top)
            w = jnp.exp2(s * SC - top[:, :1])
            o = dot(w.astype(BF), v)
            if first:
                outs.append((top, o[:, :DH], o[:, DH:]))
            else:
                fade = jnp.exp2(old - top)
                outs.append((top, acc[rows[u], :] * fade + o[:, :DH], l_s[rows[u], :] * fade + o[:, DH:]))
        for u in range(count):
            m_s[rows[u], :], acc[rows[u], :], l_s[rows[u], :] = outs[u]

    got_k(s_sib)
    got_v(s_sib)
    prefill_chunk(chip, True)

    got_k(s_zz)
    send_k(s_zz, s_x, 30).start()
    got_v(s_zz)
    send_v(s_zz, s_x, 31).start()
    to_sib(4, True)

    for p in (p_yp, p_bm, (tp + 4) % 8, (t_x + 4) % 8):
        got_x(p)
    accd[...] = jnp.zeros_like(accd)

    def d_step(c, _):
        xc = xd[c].reshape(STEPS * ROWS, KW)
        accd[:, : G * DH] += dot(xc, wqb[c])
        accd[:, G * DH :] += dot(xc, wkv[c])
        return 0

    lax.fori_loop(0, KC, d_step, 0)
    rid = lax.broadcasted_iota(jnp.int32, (DQ, DH), 0) % ROWS
    cl = jnp.zeros((DQ, DH), jnp.int32)
    pb = jnp.zeros((DQ, DH), jnp.int32)
    for r in range(ROWS):
        cl = jnp.where(rid == r, clen[r], cl)
        pb = jnp.where(rid == r, pblk[r], pb)
    n_new = STEPS * ROWS
    step_of = lax.broadcasted_iota(jnp.int32, (n_new, DH), 0) // ROWS
    dpos = (pb[:n_new] * TOK + cl[:n_new] + step_of).astype(F32)
    dcos = jnp.cos(dpos * fr)
    dsin = jnp.sin(dpos * fr) * sign
    for g in range(G):
        qd[pl.ds(g * n_new, n_new), :] = rope(accd[:, g * DH : (g + 1) * DH], dcos, dsin).astype(BF)
    kd[...] = rope(accd[:, G * DH : (G + 1) * DH], dcos, dsin).astype(BF)
    vd[:, pl.ds(0, DH)] = accd[:, (G + 1) * DH :].astype(BF)
    in_ck.wait()
    in_cv.wait()

    q = qd[...]
    row = lax.broadcasted_iota(jnp.int32, (DQ, n_new), 0)
    col = lax.broadcasted_iota(jnp.int32, (DQ, n_new), 1)
    keep = (row % ROWS == col % ROWS) & (col // ROWS <= (row % n_new) // ROWS)
    s = jnp.where(keep, scores(q, kd[...]), NEG)
    d_m = jnp.broadcast_to(jnp.max(s, axis=1, keepdims=True) * SC, (DQ, DH))
    w = jnp.exp2(s * SC - d_m[:, :1])
    d_o = dot(w.astype(BF), vd[...])

    at_once = 4
    row = lax.broadcasted_iota(jnp.int32, (DQ, at_once * 256), 0) % ROWS
    col = lax.broadcasted_iota(jnp.int32, (DQ, at_once * 256), 1)
    live = (col % 256) < cl[:, :1]
    for j in range(ROWS // at_once):
        kc = ckb[pl.ds(j * at_once, at_once)].reshape(at_once * 256, DH)
        vc = cvb[pl.ds(j * at_once, at_once)].reshape(at_once * 256, 2 * DH)
        keep = live & (col // 256 + j * at_once == row)
        s = jnp.where(keep, scores(q, kc), NEG)
        top = jnp.maximum(d_m, jnp.max(s, axis=1, keepdims=True) * SC)
        w = jnp.exp2(s * SC - top[:, :1])
        fade = jnp.exp2(d_m - top)
        d_o = d_o * jnp.concatenate([fade, fade], axis=1) + dot(w.astype(BF), vc)
        d_m = top
    dm = pl.ds(G * TOK, DQ)
    m_s[dm, :] = d_m
    acc[dm, :] = d_o[:, :DH]
    l_s[dm, :] = d_o[:, DH:]

    def chunk_step(n, _):
        dxl = jnp.where((n == 3) | (n >= 5), 1, 0)
        dz = jnp.where((n == 1) | (n == 5), 3, jnp.where((n == 2) | (n == 6), 1, jnp.where(n == 3, 0, 2)))
        c = at(dxl, dz)

        @pl.when(n == 3)
        def _():
            for i in (5, 6):
                b = at(*order[i]) * 2 + core
                got_k(b)
                got_v(b)
                to_sib(i, True)

        @pl.when(n == 4)
        def _():
            b = at(*order[7]) * 2 + core
            got_k(b)
            got_v(b)
            to_sib(7, True)

        b = 2 * c + 1 - core
        got_k(b)
        got_v(b)

        @pl.when(c < chip)
        def _():
            prefill_chunk(c, False)

        return 0

    lax.fori_loop(1, 8, chunk_step, 0)

    def dec_step(j, _):
        q = qd[...]
        d_m, d_a, d_l = m_s[dm, :], acc[dm, :], l_s[dm, :]
        for i in range(4):
            c = j * 4 + i
            k = kall[pl.ds(2 * c, 2)].reshape(2 * TOK, DH)
            v = vall[pl.ds(2 * c, 2)].reshape(2 * TOK, 2 * DH)
            s = scores(q, k)
            in0 = pb > 2 * c
            in1 = pb > 2 * c + 1
            top0 = jnp.max(s[:, :TOK], axis=1, keepdims=True) * SC
            top1 = jnp.max(s[:, TOK:], axis=1, keepdims=True) * SC
            top = jnp.maximum(d_m, jnp.maximum(jnp.where(in0, top0, NEG), jnp.where(in1, top1, NEG)))
            w0 = jnp.exp2(s[:, :TOK] * SC - jnp.where(in0, top, BIG)[:, :1])
            w1 = jnp.exp2(s[:, TOK:] * SC - jnp.where(in1, top, BIG)[:, :1])
            fade = jnp.exp2(d_m - top)
            o = dot(w0.astype(BF), v[:TOK]) + dot(w1.astype(BF), v[TOK:])
            d_a = d_a * fade + o[:, :DH]
            d_l = d_l * fade + o[:, DH:]
            d_m = top
        m_s[dm, :] = d_m
        acc[dm, :] = d_a
        l_s[dm, :] = d_l
        return 0

    lax.fori_loop(0, 2, dec_step, 0)
    d_out = (acc[dm, :] / l_s[dm, :]).astype(BF)
    for g in range(G):
        do[:, :, g * DH : (g + 1) * DH] = d_out[g * n_new : (g + 1) * n_new].reshape(STEPS, ROWS, DH)
    for g in range(G):
        r = pl.ds(g * TOK, TOK)
        po[:, g * DH : (g + 1) * DH] = (acc[r, :] / l_s[r, :]).astype(BF)

    for i, dev in enumerate((s_zp, s_zm, s_x, s_sib)):
        send_k(seq, dev, i).wait_send()
    for i, dev in enumerate((s_zm, s_zp, s_x, s_sib)):
        send_v(seq, dev, 4 + i).wait_send()
    send_k(s_zm, s_zp, 8).wait_send()
    send_v(s_zp, s_zm, 9).wait_send()
    send_k(s_x, s_zm, 10).wait_send()
    send_k(s_x, s_zp, 11).wait_send()
    send_v(s_x, s_zm, 12).wait_send()
    send_v(s_x, s_zp, 13).wait_send()
    send_k(s_zz, s_x, 30).wait_send()
    send_v(s_zz, s_x, 31).wait_send()
    for n in range(1, 8):
        to_sib(n, False)
    for cp in x_first + x_second + [x_third, x_fourth]:
        cp.wait_send()


def body(px, wq, wk, wv, dx, ck, cv, clen, pblk):
    index = np.arange(DH) % HALF
    freq = np.exp(index * (-2.0 / DH) * math.log(THETA)).astype(np.float32).reshape(1, DH)
    any_spec = pl.BlockSpec(memory_space=pl.ANY)
    smem = pl.BlockSpec(memory_space=pltpu.SMEM)
    vmem = pl.BlockSpec(memory_space=pltpu.VMEM)
    dma = pltpu.SemaphoreType.DMA
    return pl.pallas_call(
        kernel,
        name="layer",
        out_shape=(
            jax.ShapeDtypeStruct((TOK, G * DH), BF),
            jax.ShapeDtypeStruct((STEPS, ROWS, G * DH), BF),
        ),
        in_specs=[any_spec] * 7 + [smem, smem, vmem],
        out_specs=(vmem, vmem),
        scratch_shapes=[
            pltpu.VMEM((KC, TOK, KW), BF),
            pltpu.VMEM((KC, KW, 2 * DH), BF),
            pltpu.VMEM((KC, KW, G * DH), BF),
            pltpu.VMEM((16, TOK, DH), BF),
            pltpu.VMEM((16, TOK, 2 * DH), BF),
            pltpu.VMEM((8, STEPS, ROWS, KW), BF),
            pltpu.VMEM((ROWS, 256, DH), BF),
            pltpu.VMEM((ROWS, 256, 2 * DH), BF),
            pltpu.VMEM((G * TOK, DH), BF),
            pltpu.VMEM((DQ, DH), BF),
            pltpu.VMEM((STEPS * ROWS, DH), BF),
            pltpu.VMEM((STEPS * ROWS, 2 * DH), BF),
            pltpu.VMEM((G * TOK + DQ, DH), F32),
            pltpu.VMEM((G * TOK + DQ, DH), F32),
            pltpu.VMEM((G * TOK + DQ, DH), F32),
            pltpu.VMEM((TOK, G * DH), F32),
            pltpu.VMEM((TOK, 2 * DH), F32),
            pltpu.VMEM((STEPS * ROWS, (G + 2) * DH), F32),
            pltpu.VMEM((TOK, DH), F32),
            pltpu.VMEM((TOK, DH), F32),
            dma((KC,)), dma((KC,)), dma((KC,)), dma((KC,)), dma((2,)), dma,
            dma((32,)), dma((16,)), dma((16,)), dma((7,)), dma((8,)),
        ],
        compiler_params=pltpu.CompilerParams(
            collective_id=0, has_side_effects=True, vmem_limit_bytes=60 * 2**20
        ),
        cost_estimate=pl.CostEstimate(flops=20 * 10**9, bytes_accessed=26 * 10**6, transcendentals=10**7),
    )(px, wq, wk, wv, dx, ck, cv, clen, pblk, jnp.asarray(freq))


def solution(mesh):
    placed = (
        P("seq", None),
        P(None, "tp"),
        P(None, "tp"),
        P(None, "tp"),
        P(None, "seq", "tp"),
        P("seq", None, "tp"),
        P("seq", None, "tp"),
        P("seq"),
        P("seq"),
    )
    return jax.shard_map(
        body,
        mesh=mesh,
        in_specs=placed,
        out_specs=(P("seq", "tp"), P(None, "seq", "tp")),
        check_vma=False,
    )
```

time: 202 us -> 59.2 us (0.29)
  the two profiles are of different devices: /device:TPU:1 before, /device:TPU:102 now
where the time goes in v1:
time: 59.2 us; the launch traced here: 59 us
  Pallas kernels  55 us (93%)
  local copies, waits for them, and re-layouts  3.34 us (6%)
  between operations  0.64 us (1%)
    pallas_call x1, Pallas kernels, body(): pl.pallas_call(kernel, name='layer', out_shape=(jax.ShapeDtypeStruct((TOK...  55 us
    unnamed x2, local copies, waits for them, and re-layouts  3.34 us

profile of v1, /device:TPU:102, one launch (start us, length us, event | category | flops | bytes accessed | tf_op | source)
XLA Modules:
  0.0 59.0 jit_solution(1625331249791910718)
XLA Ops:
  0.6 55.0 %layer.1 = (bf16[512,512]{1,0:T(8,128)(2,1)}, bf16[4,16,512]{2,1,0:T(8,128)(2,1)}) custom-call(bf16[512,8192]{1,0:T(8,128)(2,1)} %px.1, bf16[8192,512]{1,0:T(8,128)(2,1)} %wq.1, bf16[8192,128]{1,0:T(8,128)(2,1)} %wk.1, bf16[8192,128]{1,0:T(8,128)(2,1)} %wv.1, bf16[4,16,1024]{2,1,0:T(8,128)(2,1)} %dx.1, bf16[16,256,128]{2,1,0:T(8,128)(2,1)} %ck.1, ...), custom_call_target="tpu_custom_call" | custom-call | flops 20000000000 | bytes 26000000 | tf_op jit(solution)/shard_map/layer/pallas_call | solution.py:400
  55.6 1.9 %copy.14 = bf16[512,512]{1,0:T(8,128)(2,1)} copy(bf16[512,512]{1,0:T(8,128)(2,1)} %get-tuple-element.4) | data formatting | bytes 1048576
  57.5 1.5 %copy.15 = bf16[4,16,512]{2,1,0:T(8,128)(2,1)} copy(bf16[4,16,512]{2,1,0:T(8,128)(2,1)} %get-tuple-element.5) | data formatting | bytes 131072

commit v2 on v1

v2 whole, which is shorter than its diff:
```python
import functools
import math

import jax
import jax.numpy as jnp
import numpy as np
from jax import lax
from jax.experimental import pallas as pl
from jax.experimental.pallas import tpu as pltpu
from jax.sharding import PartitionSpec as P

G = 4
DH = 128
HALF = DH // 2
TOK = 512
KC = 4
KW = 2048
XP = 8
XW = 1024
ROWS = 16
STEPS = 4
DQ = STEPS * ROWS * G
TILE = 256
THETA = 500000.0
NEG = -1e30
BIG = 1e30
SC = DH**-0.5 * math.log2(math.e)
BF = jnp.bfloat16
F32 = jnp.float32
MESH = pl.DeviceIdType.MESH


def rope(a, cos, sin):
    return a * cos + pltpu.roll(a, HALF, axis=1) * sin


def dot(a, b):
    return jnp.dot(a, b, preferred_element_type=F32)


def scores(q, k):
    return lax.dot_general(q, k, (((1,), (1,)), ((), ())), preferred_element_type=F32)


def kernel(
    px, wq, wk, wv, dx, ck, cv, clen, pblk, freq, po, do,
    xb, wkv, wqb, kall, vall, xd, ckb, cvb, qs, kd, vd,
    m_s, l_s, acc, accq, acckv, accd, cos_s, sin_s, dlim, ob,
    sx, swk, swv, swq, sc, sdx, ss, rk, rv, ssx, rx, sq, rq,
):
    seq = lax.axis_index("seq")
    tp = lax.axis_index("tp")
    core = seq % 2
    chip = seq // 2
    z = chip % 4
    xl = chip // 4

    def at(dxl, dz):
        return ((xl + dxl) % 2) * 4 + (z + dz) % 4

    s_zm = at(0, 3) * 2 + core
    s_zp = at(0, 1) * 2 + core
    s_x = at(1, 0) * 2 + core
    s_zz = at(0, 2) * 2 + core
    s_sib = chip * 2 + (1 - core)
    t_x = (tp // 2) * 2 + (1 - tp % 2)
    t_ym = (tp + 6) % 8
    t_yp = (tp + 2) % 8

    heavy = xl == 1
    mirror = 15 - seq
    far = jnp.where(heavy, chip, 7 - chip)
    give = far - 3
    order = ((0, 0), (0, 3), (0, 1), (1, 0), (0, 2), (1, 3), (1, 1), (1, 2))

    def in_x(c):
        return pltpu.make_async_copy(px.at[:, pl.ds(c * KW, KW)], xb.at[c], sx.at[c])

    def in_wk(c):
        return pltpu.make_async_copy(wk.at[pl.ds(c * KW, KW)], wkv.at[c, :, pl.ds(0, DH)], swk.at[c])

    def in_wv(c):
        return pltpu.make_async_copy(wv.at[pl.ds(c * KW, KW)], wkv.at[c, :, pl.ds(DH, DH)], swv.at[c])

    def in_wq(c):
        return pltpu.make_async_copy(wq.at[pl.ds(c * KW, KW)], wqb.at[c], swq.at[c])

    in_ck = pltpu.make_async_copy(ck, ckb, sc.at[0])
    in_cv = pltpu.make_async_copy(cv, cvb.at[:, :, pl.ds(0, DH)], sc.at[1])
    in_dx = pltpu.make_async_copy(dx, xd.at[tp], sdx)

    barrier = pltpu.get_barrier_semaphore()
    for dev in ((s_zm, tp), (s_zp, tp), (s_x, tp), (s_sib, tp), (seq, t_x), (seq, t_ym), (seq, t_yp), (mirror, tp)):
        pl.semaphore_signal(barrier, inc=1, device_id=dev, device_id_type=MESH)
    in_dx.start()
    for c in range(KC):
        in_x(c).start()
        in_wk(c).start()
        in_wv(c).start()

    def send_x(p, dev, i):
        return pltpu.make_async_remote_copy(
            src_ref=xd.at[p], dst_ref=xd.at[p], send_sem=ssx.at[i], recv_sem=rx.at[p],
            device_id=(seq, dev), device_id_type=MESH,
        )

    def send_k(b, dev, i):
        return pltpu.make_async_remote_copy(
            src_ref=kall.at[b], dst_ref=kall.at[b], send_sem=ss.at[i], recv_sem=rk.at[b],
            device_id=(dev, tp), device_id_type=MESH,
        )

    def send_v(b, dev, i):
        ref = vall.at[b, :, pl.ds(0, DH)]
        return pltpu.make_async_remote_copy(
            src_ref=ref, dst_ref=ref, send_sem=ss.at[i], recv_sem=rv.at[b],
            device_id=(dev, tp), device_id_type=MESH,
        )

    def got_k(b):
        send_k(b, s_sib, 0).wait_recv()

    def got_v(b):
        send_v(b, s_sib, 0).wait_recv()

    in_dx.wait()
    pl.semaphore_wait(barrier, 8)
    p_x, p_ym, p_yp = t_x, t_ym, t_yp
    x_first = [send_x(tp, t_x, 0), send_x(tp, t_yp, 1), send_x(tp, t_ym, 2)]
    for cp in x_first:
        cp.start()

    arrival = [at(dxl, dz) for dxl, dz in order]

    def ranks(top):
        found, out = 0, []
        for c in arrival:
            out.append(jnp.where(c <= top, found, 99))
            found = found + jnp.where(c <= top, 1, 0)
        return out

    own_rank = ranks(chip)
    far_rank = ranks(far)

    lane = lax.broadcasted_iota(jnp.int32, (1, DH), 1)
    sign = jnp.where(lane < HALF, -1.0, 1.0).astype(F32)
    fr = freq[...]
    pos = (lax.broadcasted_iota(jnp.int32, (TOK, DH), 0) + seq * TOK).astype(F32)
    cos_s[...] = jnp.cos(pos * fr)
    sin_s[...] = jnp.sin(pos * fr) * sign
    vall[:, :, pl.ds(DH, DH)] = jnp.ones((16, TOK, DH), BF)
    cvb[:, :, pl.ds(DH, DH)] = jnp.ones((ROWS, 256, DH), BF)
    vd[:, pl.ds(DH, DH)] = jnp.ones((STEPS * ROWS, DH), BF)

    rid = lax.broadcasted_iota(jnp.int32, (DQ, DH), 0) % ROWS
    pb = jnp.zeros((DQ, DH), jnp.int32)
    for r in range(ROWS):
        pb = jnp.where(rid == r, pblk[r], pb)
    dlim[...] = pb * TOK
    qs[pl.ds(13 * TILE, TILE), :] = jnp.zeros((TILE, DH), BF)
    acckv[...] = jnp.zeros_like(acckv)

    def kv_step(c, _):
        in_x(c).wait()
        in_wk(c).wait()
        in_wv(c).wait()

        @pl.when(c >= KC // 2)
        def _():
            in_wq(2 * c - KC).start()
            in_wq(2 * c - KC + 1).start()

        acckv[...] += dot(xb[c], wkv[c])
        return 0

    lax.fori_loop(0, KC, kv_step, 0)
    in_ck.start()
    in_cv.start()
    kall[seq] = rope(acckv[:, :DH], cos_s[...], sin_s[...]).astype(BF)
    vall[seq, :, pl.ds(0, DH)] = acckv[:, DH:].astype(BF)
    for i, dev in enumerate((s_zp, s_zm, s_x, s_sib)):
        send_k(seq, dev, i).start()
    for i, dev in enumerate((s_zm, s_zp, s_x, s_sib)):
        send_v(seq, dev, 4 + i).start()

    got_x = lambda p: send_x(p, t_x, 0).wait_recv()
    got_x(p_x)
    x_second = [send_x(p_x, t_yp, 3), send_x(p_x, t_ym, 4)]
    for cp in x_second:
        cp.start()
    got_x(p_ym)
    x_third = send_x(p_ym, t_yp, 5)
    x_third.start()

    accq[...] = jnp.zeros_like(accq)

    def q_rope(g):
        qs[pl.ds(g * TOK, TOK), :] = rope(
            accq[:, g * DH : (g + 1) * DH], cos_s[...], sin_s[...]
        ).astype(BF)

    def q_step(c, _):
        in_wq(c).wait()
        accq[...] += dot(xb[c], wqb[c])
        return 0

    lax.fori_loop(0, KC, q_step, 0)
    for g in range(G):
        q_rope(g)

    def tile_rows(t):
        return pl.ds(pl.multiple_of(t * TILE, TILE), TILE)

    def send_q(g):
        return pltpu.make_async_remote_copy(
            src_ref=qs.at[tile_rows(8 - give + g)], dst_ref=qs.at[tile_rows(8 + g)],
            send_sem=sq.at[g], recv_sem=rq.at[g], device_id=(mirror, tp), device_id_type=MESH,
        )

    def send_o(g):
        return pltpu.make_async_remote_copy(
            src_ref=ob.at[g], dst_ref=ob.at[g],
            send_sem=sq.at[g], recv_sem=rq.at[g], device_id=(mirror, tp), device_id_type=MESH,
        )

    for g in range(4):

        @pl.when(heavy & (give > g))
        def _(g=g):
            send_q(g).start()

    p_bp = (t_yp // 2) * 2 + (1 - tp % 2)
    p_bm = (t_ym // 2) * 2 + (1 - tp % 2)
    got_k(s_zm)
    send_k(s_zm, s_zp, 8).start()
    got_k(s_x)
    send_k(s_x, s_zm, 10).start()
    send_k(s_x, s_zp, 11).start()
    got_x(p_bp)
    x_fourth = send_x(p_bp, t_ym, 6)
    x_fourth.start()

    def core_block(n):
        return at(*order[n]) * 2 + core

    def to_sib(n, start):
        b = core_block(n)
        for cp in (send_k(b, s_sib, 14 + 2 * n), send_v(b, s_sib, 15 + 2 * n)):
            if start:
                cp.start()
            else:
                cp.wait_send()

    def from_sib(n):
        b = at(*order[n]) * 2 + 1 - core
        got_k(b)
        got_v(b)

    m_s[...] = jnp.full_like(m_s, NEG)
    l_s[...] = jnp.zeros_like(l_s)
    acc[...] = jnp.zeros_like(acc)
    from_sib(0)

    n_new = STEPS * ROWS
    dm = pl.ds(12 * TILE, TILE)

    def decode_project():
        for p in (p_yp, p_bm, (tp + 4) % 8, (t_x + 4) % 8):
            got_x(p)
        accd[...] = jnp.zeros_like(accd)

        def d_step(c, _):
            xc = xd[c].reshape(STEPS * ROWS, XW)
            r = pl.ds(pl.multiple_of(c % 2 * XW, XW), XW)
            accd[:, : G * DH] += dot(xc, wqb[c // 2, r, :])
            accd[:, G * DH :] += dot(xc, wkv[c // 2, r, :])
            return 0

        lax.fori_loop(0, XP, d_step, 0)

    def decode_local():
        cl = jnp.zeros((DQ, DH), jnp.int32)
        for r in range(ROWS):
            cl = jnp.where(rid == r, clen[r], cl)
        step_of = lax.broadcasted_iota(jnp.int32, (n_new, DH), 0) // ROWS
        dpos = (dlim[:n_new, :] + cl[:n_new] + step_of).astype(F32)
        dcos = jnp.cos(dpos * fr)
        dsin = jnp.sin(dpos * fr) * sign
        for g in range(G):
            qs[pl.ds(12 * TILE + g * n_new, n_new), :] = rope(
                accd[:, g * DH : (g + 1) * DH], dcos, dsin
            ).astype(BF)
        kd[...] = rope(accd[:, G * DH : (G + 1) * DH], dcos, dsin).astype(BF)
        vd[:, pl.ds(0, DH)] = accd[:, (G + 1) * DH :].astype(BF)
        in_ck.wait()
        in_cv.wait()

        q = qs[dm, :]
        row = lax.broadcasted_iota(jnp.int32, (DQ, n_new), 0)
        col = lax.broadcasted_iota(jnp.int32, (DQ, n_new), 1)
        keep = (row % ROWS == col % ROWS) & (col // ROWS <= (row % n_new) // ROWS)
        s = jnp.where(keep, scores(q, kd[...]), NEG)
        d_m = jnp.broadcast_to(jnp.max(s, axis=1, keepdims=True) * SC, (DQ, DH))
        w = jnp.exp2(s * SC - d_m[:, :1])
        d_o = dot(w.astype(BF), vd[...])

        at_once = 4
        row = lax.broadcasted_iota(jnp.int32, (DQ, at_once * 256), 0) % ROWS
        col = lax.broadcasted_iota(jnp.int32, (DQ, at_once * 256), 1)
        live = (col % 256) < cl[:, :1]
        for j in range(ROWS // at_once):
            kc = ckb[pl.ds(j * at_once, at_once)].reshape(at_once * 256, DH)
            vc = cvb[pl.ds(j * at_once, at_once)].reshape(at_once * 256, 2 * DH)
            keep = live & (col // 256 + j * at_once == row)
            s = jnp.where(keep, scores(q, kc), NEG)
            top = jnp.maximum(d_m, jnp.max(s, axis=1, keepdims=True) * SC)
            w = jnp.exp2(s * SC - top[:, :1])
            fade = jnp.exp2(d_m - top)
            d_o = d_o * jnp.concatenate([fade, fade], axis=1) + dot(w.astype(BF), vc)
            d_m = top
        m_s[dm, :] = d_m
        acc[dm, :] = d_o[:, :DH]
        l_s[dm, :] = d_o[:, DH:]

    def give_back(g):
        @pl.when(~heavy & (give > g))
        def _():
            r = tile_rows(8 + g)
            ob[g] = (acc[r, :] / l_s[r, :]).astype(BF)
            send_o(g).start()

    tiles = jnp.where(heavy, 8 - give, 8)
    stride = jnp.where(tiles == 7, 8, tiles)
    own_rest = stride * chip
    before = jnp.where(heavy, own_rest, 8 * (jnp.maximum(chip, 1) - 1))
    given = jnp.where(heavy, 0, give * (far + 1))
    row_i = lax.broadcasted_iota(jnp.int32, (TILE, DH), 0)
    col_i = lax.broadcasted_iota(jnp.int32, (TILE, 2 * TOK), 1)

    def wide(a):
        return jnp.concatenate([a] * (2 * TOK // DH), axis=1)

    def item(blk, u):
        i = (blk - 1) * 8 + u
        is_given = (i >= before) & (i < before + given)
        j = jnp.maximum(jnp.where(i >= before + given, i - given, i), 0)
        k = jnp.maximum(i - before, 0)
        late = (give == 4) & (k >= 16)
        g_tile = jnp.where(late, (k // 8 - 2) * 2 + k % 2, k % give)
        g_spot = jnp.where(late, 4 + (k % 8) // 2, k // give)
        t = jnp.where(is_given, 8 + g_tile, j % stride)
        spot = jnp.where(is_given, g_spot, 1 + j // stride)
        none = (i >= own_rest + given) | (~is_given & (j % stride >= tiles))
        first = blk == 0
        last = blk == 5
        t = jnp.where(first, u, jnp.where(last, 12, jnp.where(none, 13, t)))
        t = jnp.where(first & (u >= tiles), 13, t)
        c = chip
        for n in range(1, 8):
            rank = jnp.where(is_given, far_rank[n], own_rank[n])
            c = jnp.where(rank == spot, arrival[n], c)
        c = jnp.where(first | none, chip, c)
        c = jnp.where(last, u, c)
        mine = chip * 1024 + core * TOK + (t % 2) * TILE
        theirs = far * 1024 + (1 - core) * TOK + ((t - give) % 2) * TILE
        start = jnp.where(t < 8, mine, jnp.where(t < 12, theirs, -(2**20))) - c * 1024 + 1
        return t, c, start

    def block(blk):
        items = [item(blk, u) for u in range(8)]

        def item_scores(u):
            t, c, _ = items[u]
            return scores(qs[tile_rows(t), :], kall[pl.ds(2 * c, 2)].reshape(2 * TOK, DH))

        s_next = item_scores(0)
        outs = []
        for u in range(8):
            s = s_next
            if u < 7:
                s_next = item_scores(u + 1)
            t, c, start = items[u]
            lim = jnp.where(t == 12, dlim[...] - c * 1024, row_i + start)
            s = jnp.where(col_i < wide(lim), s, NEG)
            top = jnp.broadcast_to(jnp.max(s, axis=1, keepdims=True) * SC, (TILE, DH))
            w = jnp.exp2(s * SC - wide(top))
            outs.append((top, dot(w.astype(BF), vall[pl.ds(2 * c, 2)].reshape(2 * TOK, 2 * DH))))
        for u in range(8):
            r = tile_rows(items[u][0])
            top, o = outs[u]
            old = m_s[r, :]
            new = jnp.maximum(old, top)
            fade = jnp.exp2(old - new)
            part = jnp.exp2(top - new)
            m_s[r, :] = new
            acc[r, :] = acc[r, :] * fade + o[:, :DH] * part
            l_s[r, :] = l_s[r, :] * fade + o[:, DH:] * part

    def take(n):
        b = core_block(n)
        got_k(b)
        got_v(b)
        to_sib(n, True)

    def from_three():
        for n in (1, 2, 3):
            from_sib(n)

    def phase(ph, _):
        @pl.when(ph == 1)
        def _():
            got_v(s_zp)
            send_v(s_zp, s_zm, 9).start()
            got_v(s_x)
            send_v(s_x, s_zm, 12).start()
            send_v(s_x, s_zp, 13).start()
            got_v(s_zm)
            got_k(s_zp)
            for n in (1, 2, 3):
                to_sib(n, True)

            @pl.when(heavy)
            def _():
                from_three()

        @pl.when(ph == 2)
        def _():
            got_k(s_zz)
            send_k(s_zz, s_x, 30).start()
            got_v(s_zz)
            send_v(s_zz, s_x, 31).start()
            to_sib(4, True)

            @pl.when(~heavy)
            def _():
                from_three()

            for g in range(4):

                @pl.when(~heavy & (give > g))
                def _(g=g):
                    send_q(g).wait_recv()

        @pl.when(ph == 3)
        def _():
            take(5)
            take(6)
            from_sib(4)
            from_sib(5)

        @pl.when(ph == 4)
        def _():
            take(7)
            from_sib(6)

        soon = (chip == 0) | (chip == 2)

        @pl.when(soon & (ph == 4) | ~soon & (ph == 5))
        def _():
            from_sib(7)

        decoding = ph == jnp.where(heavy, 2, 1)

        @pl.when(decoding)
        def _():
            decode_project()
            decode_local()

        @pl.when(~decoding)
        def _():
            block(jnp.where(ph > jnp.where(heavy, 2, 1), ph - 1, ph))

        @pl.when(ph == 4)
        def _():
            give_back(0)
            give_back(1)

            @pl.when(give == 3)
            def _():
                give_back(2)

        @pl.when((ph == 5) & (give == 4))
        def _():
            give_back(2)
            give_back(3)

        return 0

    lax.fori_loop(0, 7, phase, 0)
    d_out = (acc[dm, :] / l_s[dm, :]).astype(BF)
    for g in range(G):
        do[:, :, g * DH : (g + 1) * DH] = d_out[g * n_new : (g + 1) * n_new].reshape(STEPS, ROWS, DH)

    def put(t, o):
        po[(t % 2) * TILE : (t % 2 + 1) * TILE, (t // 2) * DH : (t // 2 + 1) * DH] = o

    for t in range(8):
        own = ~(heavy & (t >= 8 - give))

        @pl.when(own)
        def _(t=t):
            put(t, (acc[tile_rows(t), :] / l_s[tile_rows(t), :]).astype(BF))

    for g in range(4):

        @pl.when(heavy & (give > g))
        def _(g=g):
            send_o(g).wait_recv()

    for t in range(4, 8):

        @pl.when(heavy & (t >= 8 - give))
        def _(t=t):
            put(t, ob[t - 8 + give])

    for g in range(4):

        @pl.when(give > g)
        def _(g=g):
            send_o(g).wait_send()

    for i, dev in enumerate((s_zp, s_zm, s_x, s_sib)):
        send_k(seq, dev, i).wait_send()
    for i, dev in enumerate((s_zm, s_zp, s_x, s_sib)):
        send_v(seq, dev, 4 + i).wait_send()
    send_k(s_zm, s_zp, 8).wait_send()
    send_v(s_zp, s_zm, 9).wait_send()
    send_k(s_x, s_zm, 10).wait_send()
    send_k(s_x, s_zp, 11).wait_send()
    send_v(s_x, s_zm, 12).wait_send()
    send_v(s_x, s_zp, 13).wait_send()
    send_k(s_zz, s_x, 30).wait_send()
    send_v(s_zz, s_x, 31).wait_send()
    for n in range(1, 8):
        to_sib(n, False)
    for cp in x_first + x_second + [x_third, x_fourth]:
        cp.wait_send()


def move(p_in, d_in, p_out, d_out):
    p_out[...] = p_in[...]
    d_out[...] = d_in[...]


def body(px, wq, wk, wv, dx, ck, cv, clen, pblk):
    index = np.arange(DH) % HALF
    freq = np.exp(index * (-2.0 / DH) * math.log(THETA)).astype(np.float32).reshape(1, DH)
    any_spec = pl.BlockSpec(memory_space=pl.ANY)
    smem = pl.BlockSpec(memory_space=pltpu.SMEM)
    vmem = pl.BlockSpec(memory_space=pltpu.VMEM)
    dma = pltpu.SemaphoreType.DMA
    raw = pl.pallas_call(
        kernel,
        name="layer",
        out_shape=(
            jax.ShapeDtypeStruct((TOK, G * DH), BF),
            jax.ShapeDtypeStruct((STEPS, ROWS, G * DH), BF),
        ),
        in_specs=[any_spec] * 7 + [smem, smem, vmem],
        out_specs=(vmem, vmem),
        scratch_shapes=[
            pltpu.VMEM((KC, TOK, KW), BF),
            pltpu.VMEM((KC, KW, 2 * DH), BF),
            pltpu.VMEM((KC, KW, G * DH), BF),
            pltpu.VMEM((16, TOK, DH), BF),
            pltpu.VMEM((16, TOK, 2 * DH), BF),
            pltpu.VMEM((XP, STEPS, ROWS, XW), BF),
            pltpu.VMEM((ROWS, 256, DH), BF),
            pltpu.VMEM((ROWS, 256, 2 * DH), BF),
            pltpu.VMEM((14 * TILE, DH), BF),
            pltpu.VMEM((STEPS * ROWS, DH), BF),
            pltpu.VMEM((STEPS * ROWS, 2 * DH), BF),
            pltpu.VMEM((14 * TILE, DH), F32),
            pltpu.VMEM((14 * TILE, DH), F32),
            pltpu.VMEM((14 * TILE, DH), F32),
            pltpu.VMEM((TOK, G * DH), F32),
            pltpu.VMEM((TOK, 2 * DH), F32),
            pltpu.VMEM((STEPS * ROWS, (G + 2) * DH), F32),
            pltpu.VMEM((TOK, DH), F32),
            pltpu.VMEM((TOK, DH), F32),
            pltpu.VMEM((DQ, DH), jnp.int32),
            pltpu.VMEM((4, TILE, DH), BF),
            dma((KC,)), dma((KC,)), dma((KC,)), dma((KC,)), dma((2,)), dma,
            dma((32,)), dma((16,)), dma((16,)), dma((7,)), dma((8,)), dma((4,)), dma((4,)),
        ],
        compiler_params=pltpu.CompilerParams(
            collective_id=0, has_side_effects=True, vmem_limit_bytes=60 * 2**20
        ),
        cost_estimate=pl.CostEstimate(flops=20 * 10**9, bytes_accessed=26 * 10**6, transcendentals=10**7),
    )(px, wq, wk, wv, dx, ck, cv, clen, pblk, jnp.asarray(freq))
    return pl.pallas_call(
        move,
        name="place",
        out_shape=tuple(jax.ShapeDtypeStruct(o.shape, o.dtype) for o in raw),
        in_specs=[vmem] * 2,
        out_specs=(vmem,) * 2,
    )(*raw)


def solution(mesh):
    placed = (
        P("seq", None),
        P(None, "tp"),
        P(None, "tp"),
        P(None, "tp"),
        P(None, "seq", "tp"),
        P("seq", None, "tp"),
        P("seq", None, "tp"),
        P("seq"),
        P("seq"),
    )
    return jax.shard_map(
        body,
        mesh=mesh,
        in_specs=placed,
        out_specs=(P("seq", "tp"), P(None, "seq", "tp")),
        check_vma=False,
    )
```

time: 59.2 us -> 57.3 us (0.968)
  the two profiles are of different devices: /device:TPU:102 before, /device:TPU:17 now
where the time goes in v2:
time: 57.3 us; the launch traced here: 57.1 us
  Pallas kernels  56.5 us (99%)
  between operations  0.64 us (1%)
    pallas_call x1, Pallas kernels, body(): pl.pallas_call(kernel, name='layer', out_shape=(jax.ShapeDtypeStruct((TOK...  54.6 us
    pallas_call x1, Pallas kernels, body(): pl.pallas_call(move, name='place', out_shape=tuple((jax.ShapeDtypeStruct(...  1.88 us

profile of v2, /device:TPU:17, one launch (start us, length us, event | category | flops | bytes accessed | tf_op | source)
XLA Modules:
  0.0 57.1 jit_solution(15728160479778560547)
XLA Ops:
  0.6 54.6 %layer.1 = (bf16[512,512]{1,0:T(8,128)(2,1)}, bf16[4,16,512]{2,1,0:T(8,128)(2,1)}) custom-call(bf16[512,8192]{1,0:T(8,128)(2,1)} %px.1, bf16[8192,512]{1,0:T(8,128)(2,1)} %wq.1, bf16[8192,128]{1,0:T(8,128)(2,1)} %wk.1, bf16[8192,128]{1,0:T(8,128)(2,1)} %wv.1, bf16[4,16,1024]{2,1,0:T(8,128)(2,1)} %dx.1, bf16[16,256,128]{2,1,0:T(8,128)(2,1)} %ck.1, ...), custom_call_target="tpu_custom_call" | custom-call | flops 20000000000 | bytes 26000000 | tf_op jit(solution)/shard_map/layer/pallas_call | solution.py:552
  55.3 1.9 %place.1 = (bf16[512,512]{1,0:T(8,128)(2,1)}, bf16[4,16,512]{2,1,0:T(8,128)(2,1)}) custom-call(bf16[512,512]{1,0:T(8,128)(2,1)} %get-tuple-element.4.p_in, bf16[4,16,512]{2,1,0:T(8,128)(2,1)} %get-tuple-element.5.d_in), custom_call_target="tpu_custom_call" | custom-call | tf_op jit(solution)/shard_map/place/pallas_call | solution.py:591

commit v3 on v1

--- a/solution.py
+++ b/solution.py
@@ -13,8 +13,10 @@
 DH = 128
 HALF = DH // 2
 TOK = 512
-KC = 8
-KW = 1024
+KC = 4
+KW = 2048
+XP = 8
+XW = 1024
 ROWS = 16
 STEPS = 4
 DQ = STEPS * ROWS * G
@@ -181,9 +183,6 @@
 
     p_bp = (t_yp // 2) * 2 + (1 - tp % 2)
     p_bm = (t_ym // 2) * 2 + (1 - tp % 2)
-    got_x(p_bp)
-    x_fourth = send_x(p_bp, t_ym, 6)
-    x_fourth.start()
     got_k(s_zm)
     send_k(s_zm, s_zp, 8).start()
     got_v(s_zp)
@@ -196,6 +195,9 @@
     send_v(s_x, s_zp, 13).start()
     got_v(s_zm)
     got_k(s_zp)
+    got_x(p_bp)
+    x_fourth = send_x(p_bp, t_ym, 6)
+    x_fourth.start()
     order = ((0, 0), (0, 3), (0, 1), (1, 0), (0, 2), (1, 3), (1, 1), (1, 2))
 
     def to_sib(n, start):
@@ -255,12 +257,13 @@
     accd[...] = jnp.zeros_like(accd)
 
     def d_step(c, _):
-        xc = xd[c].reshape(STEPS * ROWS, KW)
-        accd[:, : G * DH] += dot(xc, wqb[c])
-        accd[:, G * DH :] += dot(xc, wkv[c])
+        xc = xd[c].reshape(STEPS * ROWS, XW)
+        r = pl.ds(pl.multiple_of(c % 2 * XW, XW), XW)
+        accd[:, : G * DH] += dot(xc, wqb[c // 2, r, :])
+        accd[:, G * DH :] += dot(xc, wkv[c // 2, r, :])
         return 0
 
-    lax.fori_loop(0, KC, d_step, 0)
+    lax.fori_loop(0, XP, d_step, 0)
     rid = lax.broadcasted_iota(jnp.int32, (DQ, DH), 0) % ROWS
     cl = jnp.zeros((DQ, DH), jnp.int32)
     pb = jnp.zeros((DQ, DH), jnp.int32)
@@ -390,6 +393,11 @@
         cp.wait_send()
 
 
+def move(p_in, d_in, p_out, d_out):
+    p_out[...] = p_in[...]
+    d_out[...] = d_in[...]
+
+
 def body(px, wq, wk, wv, dx, ck, cv, clen, pblk):
     index = np.arange(DH) % HALF
     freq = np.exp(index * (-2.0 / DH) * math.log(THETA)).astype(np.float32).reshape(1, DH)
@@ -397,7 +405,7 @@
     smem = pl.BlockSpec(memory_space=pltpu.SMEM)
     vmem = pl.BlockSpec(memory_space=pltpu.VMEM)
     dma = pltpu.SemaphoreType.DMA
-    return pl.pallas_call(
+    raw = pl.pallas_call(
         kernel,
         name="layer",
         out_shape=(
@@ -412,7 +420,7 @@
             pltpu.VMEM((KC, KW, G * DH), BF),
             pltpu.VMEM((16, TOK, DH), BF),
             pltpu.VMEM((16, TOK, 2 * DH), BF),
-            pltpu.VMEM((8, STEPS, ROWS, KW), BF),
+            pltpu.VMEM((XP, STEPS, ROWS, XW), BF),
             pltpu.VMEM((ROWS, 256, DH), BF),
             pltpu.VMEM((ROWS, 256, 2 * DH), BF),
             pltpu.VMEM((G * TOK, DH), BF),
@@ -435,6 +443,13 @@
         ),
         cost_estimate=pl.CostEstimate(flops=20 * 10**9, bytes_accessed=26 * 10**6, transcendentals=10**7),
     )(px, wq, wk, wv, dx, ck, cv, clen, pblk, jnp.asarray(freq))
+    return pl.pallas_call(
+        move,
+        name="place",
+        out_shape=tuple(jax.ShapeDtypeStruct(o.shape, o.dtype) for o in raw),
+        in_specs=[vmem] * 2,
+        out_specs=(vmem,) * 2,
+    )(*raw)
 
 
 def solution(mesh):

time: 59.2 us -> 56.4 us (0.953)
  local copies, waits for them, and re-layouts: 3.34 us -> 0 us
  Pallas kernels: 55 us -> 55.7 us
    unnamed x2 -> x0, local copies, waits for them, and re-layouts: 3.34 us -> none
    pallas_call x0 -> x1, Pallas kernels: none -> 1.88 us  [body(): pl.pallas_call(move, name='place', out_shape=tuple((jax.ShapeDtypeStruct(...]
    pallas_call x1, Pallas kernels: 55 us -> 53.8 us  [body(): pl.pallas_call(kernel, name='layer', out_shape=(jax.ShapeDtypeStruct((TOK...]
where the time goes in v3:
time: 56.4 us; the launch traced here: 56.3 us
  Pallas kernels  55.7 us (99%)
  between operations  0.64 us (1%)
    pallas_call x1, Pallas kernels, body(): pl.pallas_call(kernel, name='layer', out_shape=(jax.ShapeDtypeStruct((TOK...  53.8 us
    pallas_call x1, Pallas kernels, body(): pl.pallas_call(move, name='place', out_shape=tuple((jax.ShapeDtypeStruct(...  1.88 us

profile of v3, /device:TPU:102, one launch (start us, length us, event | category | flops | bytes accessed | tf_op | source)
XLA Modules:
  0.0 56.3 jit_solution(1137925231233081350)
XLA Ops:
  0.6 53.8 %layer.1 = (bf16[512,512]{1,0:T(8,128)(2,1)}, bf16[4,16,512]{2,1,0:T(8,128)(2,1)}) custom-call(bf16[512,8192]{1,0:T(8,128)(2,1)} %px.1, bf16[8192,512]{1,0:T(8,128)(2,1)} %wq.1, bf16[8192,128]{1,0:T(8,128)(2,1)} %wk.1, bf16[8192,128]{1,0:T(8,128)(2,1)} %wv.1, bf16[4,16,1024]{2,1,0:T(8,128)(2,1)} %dx.1, bf16[16,256,128]{2,1,0:T(8,128)(2,1)} %ck.1, ...), custom_call_target="tpu_custom_call" | custom-call | flops 20000000000 | bytes 26000000 | tf_op jit(solution)/shard_map/layer/pallas_call | solution.py:408
  54.4 1.9 %place.1 = (bf16[512,512]{1,0:T(8,128)(2,1)}, bf16[4,16,512]{2,1,0:T(8,128)(2,1)}) custom-call(bf16[512,512]{1,0:T(8,128)(2,1)} %get-tuple-element.4.p_in, bf16[4,16,512]{2,1,0:T(8,128)(2,1)} %get-tuple-element.5.d_in), custom_call_target="tpu_custom_call" | custom-call | tf_op jit(solution)/shard_map/place/pallas_call | solution.py:446
